TPU v7x, 512 devices: a whole 4x4x16 slice. The times are simulated.
512 devices in a mesh: cell: 64 (over z_lo, x, core), gene: 8 (over y, z_hi).
Axes of the slice: x: 4, y: 4, z: 16 (z_hi: 2, z_lo: 8; z = z_hi * 8 + z_lo), core: 2. Of those that a mesh axis runs over, the one named last changes fastest.
Arguments:
- counts: bfloat16 [61440, 16384], P('cell', 'gene'), as said below
- w_factor: float32 [61440, 128], P('cell'), may hold values from 0.004 to 2, as said below
- h_factor: float32 [128, 16384], P('cell', 'gene'), may hold values from 0.03 to 0.3, as said below
Outputs:
- w_updated: float32 [61440, 128], P('cell')
- h_updated: float32 [128, 16384], P('cell', 'gene')
Inputs may be any that keep to these rules, and one draw needn't show every extreme that they name: `counts`: nonnegative whole numbers. `w_factor`: positive. `h_factor`: positive.
All inputs are finite; a program needn't handle non-finite values.
Results may differ from a plain program's by a relative error of at most 0.00092.
Values may be sent and summed in bfloat16 or wider, within the bound.
A program may use at most 64 MiB of HBM per device.

v0:
```python
import jax
import jax.numpy as jnp
from jax import lax
from jax.sharding import PartitionSpec as P


def per_device(counts, w_factor, h_factor):
    own_rows = h_factor.shape[0]
    w_copy = w_factor.astype(jnp.bfloat16)
    row_offset = lax.axis_index("cell") * own_rows
    counts_float = counts.astype(jnp.float32)
    columns = w_copy
    modeled = jnp.dot(
        columns,
        lax.all_gather(h_factor.astype(jnp.bfloat16), "cell", axis=0, tiled=True),
        preferred_element_type=jnp.float32,
    )
    quotient = (counts_float / modeled).astype(jnp.bfloat16)
    columns = w_copy
    numerator = lax.psum_scatter(
        lax.dot_general(
            columns, quotient, (((0,), (0,)), ((), ())), preferred_element_type=jnp.float32
        ),
        "cell",
        scatter_dimension=0,
        tiled=True,
    )
    w_totals = lax.psum(jnp.sum(w_factor, axis=0), "cell")
    own_totals = lax.dynamic_slice_in_dim(w_totals, row_offset, own_rows, 0)
    h_updated = h_factor * numerator / own_totals[:, None]
    h_new_copy = lax.all_gather(h_updated.astype(jnp.bfloat16), "cell", axis=0, tiled=True)
    modeled_again = jnp.dot(w_copy, h_new_copy, preferred_element_type=jnp.float32)
    quotient_again = (counts_float / modeled_again).astype(jnp.bfloat16)
    partial_w = lax.dot_general(
        quotient_again, h_new_copy, (((1,), (1,)), ((), ())), preferred_element_type=jnp.float32
    )
    partial_totals = jnp.sum(h_new_copy.astype(jnp.float32), axis=1)
    w_numerator, h_totals = lax.psum((partial_w, partial_totals), "gene")
    w_updated = w_factor * w_numerator / h_totals[None, :]
    return (w_updated, h_updated)


def solution(mesh):
    in_specs = (P("cell", "gene"), P("cell", None), P("cell", "gene"))
    out_specs = (P("cell", None), P("cell", "gene"))
    return jax.shard_map(
        per_device, mesh=mesh, in_specs=in_specs, out_specs=out_specs, check_vma=False
    )
```

profile of v0, /device:TPU:116, one launch (start us, length us, event | category | flops | bytes accessed | tf_op | source)
XLA Modules:
  0.0 1275.4 jit_solution(4205563765050539474)
XLA Ops:
  7.2 0.0 all-reduce.6.cloned.1.call-start
  7.2 0.7 convert_bitcast_fusion.1
  7.9 68.6 %all-gather = bf16[64,2,2048]{2,1,0:T(2,128)(2,1)S(1)} all-gather(bf16[1,2,2048]{2,1,0:T(2,128)(2,1)S(1)} %convert_bitcast_fusion.1), channel_id=1, replica_groups=mesh['cell'=64,'gene'=8] {'cell'}, dimensions={0}, use_global_device_ids=true | all-gather | bytes 532480 | tf_op jit(solution)/shard_map/all_gather | solution.py:15
  76.5 0.2 reshape.7
  76.7 0.0 copy-start.1
  76.7 0.0 copy-start
  76.7 5.8 fusion.6
  82.6 0.0 all-reduce.6.cloned.1.call-update
  82.6 0.0 all-reduce.4.cloned.1.call-start
  82.6 0.0 copy-done.1
  82.7 0.4 copy.10
  83.0 0.0 copy-done
  83.0 0.1 reduce_sum.18
  83.2 1.3 dynamic-slice
  85.1 129.0 %psum.21 = f32[128]{0:T(128)S(1)} all-reduce(f32[128]{0:T(128)S(1)} %reduce_sum.18), channel_id=1, replica_groups=mesh['cell'=64,'gene'=8] {'cell'}, use_global_device_ids=true, to_apply=%region_2.0 | all-reduce | flops 128 | bytes 1024 | tf_op jit(solution)/shard_map/psum | solution.py:28
  214.1 0.1 dynamic_slice.3
  214.2 635.0 %all-reduce.6.cloned.1.call-done = f32[128,2048]{0,1:T(8,128)} async-done(((f32[128,2048]{0,1:T(8,128)}), f32[128,2048]{0,1:T(8,128)}) %all-reduce.6.cloned.1.call-update) | async-done | bytes 1048592
  849.2 1.6 convert_bitcast_fusion
  850.7 0.2 copy.11
  851.0 175.2 %all-gather.1 = bf16[64,2,2048]{2,1,0:T(2,128)(2,1)S(1)} all-gather(bf16[1,2,2048]{2,1,0:T(2,128)(2,1)S(1)} %copy.11), channel_id=1, replica_groups=mesh['cell'=64,'gene'=8] {'cell'}, dimensions={0}, use_global_device_ids=true | all-gather | bytes 532480 | tf_op jit(solution)/shard_map/all_gather | solution.py:31
  1026.2 0.2 reshape.9
  1026.4 5.2 fusion.9
  1031.6 0.0 all-reduce.4.cloned.1.call-update
  1031.6 0.9 copy.12
  1032.5 0.2 convert_reduce_fusion
  1032.7 34.7 %psum.23 = f32[128]{0:T(128)S(1)} all-reduce(f32[128]{0:T(128)S(1)} %convert_reduce_fusion), channel_id=1, replica_groups=mesh['cell'=64,'gene'=8] {'gene'}, use_global_device_ids=true, to_apply=%region_5.0 | all-reduce | flops 128 | bytes 1024 | tf_op jit(solution)/shard_map/psum | solution.py:38
  1067.4 199.4 %all-reduce.4.cloned.1.call-done = f32[960,128]{1,0:T(8,128)} async-done(((f32[960,128]{1,0:T(8,128)}), f32[960,128]{1,0:T(8,128)}) %all-reduce.4.cloned.1.call-update) | async-done | bytes 491536 | tf_op jit(solution)/shard_map/psum | solution.py:38
  1266.7 1.9 multiply_divide_fusion
Async XLA Ops:
  7.2 842.0 %all-reduce.6.cloned.1.call-start = ((), (), s32[]{:S(2)}) async-start(), calls=%async_computation.1 | async-start | bytes 2097152
  76.7 5.9 copy-start.1
  76.7 6.3 copy-start
  82.6 1184.2 %all-reduce.4.cloned.1.call-start = ((), (), s32[]{:S(2)}) async-start(), calls=%async_computation | async-start | bytes 983040 | tf_op jit(solution)/shard_map/psum | solution.py:38
Sparse Core Ops, SparseCore 0:
  82.7 766.4 all-reduce.5
  1031.7 234.9 all-reduce.3
where the time goes:
time: 1280 us
  waiting for transfers between devices  834 us (65%)
  blocking collectives  407 us (32%)
  between operations  14.8 us (1%)
    unnamed x3, waiting for transfers between devices  635 us
    psum x1, waiting for transfers between devices, per_device(): w_numerator, h_totals = lax.psum((partial_w, partial_totals), 'gene')  199 us
    all_gather x1, blocking collectives, per_device(): lax.all_gather(h_updated.astype(jnp.bfloat16), 'cell', axis=0, tiled=True)  175 us
    psum x1, blocking collectives, per_device(): w_totals = lax.psum(jnp.sum(w_factor, axis=0), 'cell')  129 us
    all_gather x1, blocking collectives, per_device(): lax.all_gather(h_factor.astype(jnp.bfloat16), 'cell', axis=0, tiled=True)  68.6 us
    psum x1, blocking collectives, per_device(): w_numerator, h_totals = lax.psum((partial_w, partial_totals), 'gene')  34.7 us
  transfers between devices with their start and end apart: 2, of which 2 were waited for; matrix products, arithmetic and copies ran while one was open for 0% of the time, Pallas kernels for 0%

commit v1 on v0

v1 whole, which is shorter than its diff:
```python
import jax
import jax.numpy as jnp
from jax import lax
from jax.experimental import pallas as pl
from jax.experimental.pallas import tpu as pltpu
from jax.sharding import PartitionSpec as P

MESH = pl.DeviceIdType.MESH
BF = jnp.bfloat16
F32 = jnp.float32
NC = 2
CH = 2048 // NC
ZG = CH // 8
ROWS = 240


def iota(shape, dim):
    return lax.broadcasted_iota(jnp.int32, shape, dim)


def natural(i):
    return ((i % 16) // 2) * 16 + ((i // 16) % 4) * 4 + (i // 64) * 2 + i % 2


def spread(tile, rows, columns):
    wide = jnp.concatenate([tile] * (columns // 128), axis=1) if columns > 128 else tile
    return jnp.concatenate([wide] * (rows // 8), axis=0) if rows > 8 else wide


def scale_of(value):
    rows, columns = value.shape
    top = jnp.full((8, 128), 1e-30, F32)
    for r in range(0, rows, 8):
        for c in range(0, columns, 128):
            top = jnp.maximum(top, value[r : r + 8, c : c + 128])
    return top.astype(BF)


def encode(value, scale):
    rows, columns = value.shape
    share = value * spread(32768.0 / scale.astype(F32), rows, columns)
    square = share * share
    fourth = square * square
    return (fourth * fourth).astype(BF)


def decode(code, scale16):
    rows, columns = code.shape
    unit = scale16[0:8, :].astype(F32) * (1.0 / 32768.0)
    root = jnp.sqrt(jnp.sqrt(jnp.sqrt(code.astype(F32))))
    return root * spread(unit, rows, columns)


def twice(scale):
    wide = scale.astype(F32)
    return jnp.concatenate([wide, wide], axis=0).astype(BF)


def kernel(
    cnt_hbm, w_hbm, h_in, w_out, h_out,
    cnt, wf, wp, wt, quo,
    hown, ha, hx32, hmat, fm, fr, h16, tx, tc,
    num, numr, bs, bx, bxr, tz, bz, bzr, hu, ho, outr, hmat2, hn, ht,
    wn, dy, dyr, dz, zr, da,
    ls, as_, ar, fs, frs, txs, txr, tcs, tcr,
    xs, xr, cs, cr, ns, nr, bxs, bxrs, bzs, bzrs, cz, czr, os_, ors, hts, htr,
    dys, dyrs, dzs, dzr, das, dar,
):
    c = lax.axis_index("cell")
    g = lax.axis_index("gene")
    z, x, k = c // 8, (c // 2) % 4, c % 2
    y, zh = g // 2, g % 2
    slot = k * 4 + x

    def at_z(d):
        return (((z + d) % 8) * 8 + x * 2 + k, g)

    def at_x(d):
        return (z * 8 + ((x + d) % 4) * 2 + k, g)

    def at_y(d):
        return (c, ((y + d) % 4) * 2 + zh)

    at_core = (z * 8 + x * 2 + (1 - k), g)
    at_zh = (c, y * 2 + (1 - zh))
    sent = []

    def send(src, dst, ssem, rsem, device):
        copy = pltpu.make_async_remote_copy(
            src_ref=src, dst_ref=dst, send_sem=ssem, recv_sem=rsem, device_id=device, device_id_type=MESH
        )
        copy.start()
        sent.append(copy)
        return copy

    load_cnt = pltpu.make_async_copy(cnt_hbm, cnt, ls.at[0])
    load_w = pltpu.make_async_copy(w_hbm, wf, ls.at[1])
    load_w.start()
    load_cnt.start()

    barrier = pltpu.get_barrier_semaphore()
    friends = [at_z(d) for d in range(1, 8)] + [at_x(d) for d in range(1, 4)] + [at_core]
    friends += [(c, (g + d) % 8) for d in range(1, 8)]
    for friend in friends:
        pl.semaphore_signal(barrier, inc=1, device_id=friend, device_id_type=MESH)

    h_own = h_in[...]
    hown[...] = h_own.astype(BF)
    load_w.wait()
    w_all = wf[...]
    w_sum = jnp.sum(w_all, axis=0, keepdims=True)
    fm[...] = jnp.zeros_like(fm)
    for zz in range(8):
        for n in range(NC):
            base = n * CH + zz * ZG
            fm[zz, 2 * n : 2 * n + 2, :] = h_own[:, base : base + ZG]
        fm[zz, 4:5, :] = w_sum
    pl.semaphore_wait(barrier, len(friends))

    got_a = []
    got_f = []
    for d in range(1, 8):
        got_a.append(send(hown, ha.at[z], as_.at[d - 1], ar.at[d - 1], at_z(d)))
    for d in range(1, 8):
        got_f.append(send(fm.at[(z + d) % 8], fr.at[z], fs.at[d - 1], frs.at[d - 1], at_z(d)))
    ha[z] = hown[...]
    fr[z] = fm[z]

    w_copy = w_all.astype(BF)
    pick = (iota((128, 128), 0) == natural(iota((128, 128), 1))).astype(F32).astype(BF)
    pick_t = (natural(iota((128, 128), 0)) == iota((128, 128), 1)).astype(F32).astype(BF)
    wp[...] = jnp.dot(w_copy, pick, preferred_element_type=F32).astype(BF)
    wt[...] = lax.dot_general(
        pick_t, w_copy, (((1,), (1,)), ((), ())), preferred_element_type=F32
    ).astype(BF)

    for copy in got_a:
        copy.wait_recv()
    for zz in range(8):
        hx32[2 * zz : 2 * zz + 2, :] = ha[zz].astype(F32)
    hmat[slot] = hx32[...].astype(BF)

    def fan_out(buf, phase, n):
        cols = pl.ds(n * CH, CH)
        mine = buf.at[slot, :, cols]
        got_x = [
            send(mine, mine, xs.at[phase, n, d - 1], xr.at[phase, n, d - 1], at_x(d)) for d in range(1, 4)
        ]
        got_c = [send(mine, mine, cs.at[phase, n, 0], cr.at[phase, n, 0], at_core)]
        return got_x, got_c

    def fan_on(buf, phase, n, got):
        cols = pl.ds(n * CH, CH)
        for d in (1, 3, 2):
            got[0][d - 1].wait_recv()
            piece = buf.at[k * 4 + (x + 4 - d) % 4, :, cols]
            got[1].append(send(piece, piece, cs.at[phase, n, d], cr.at[phase, n, d], at_core))

    def fan_in(got):
        for copy in got[1]:
            copy.wait_recv()

    got = [fan_out(hmat, 0, n) for n in range(NC)]

    for copy in got_f:
        copy.wait_recv()
    tot = jnp.zeros((1, 128), F32)
    for zz in range(8):
        tot = tot + fr[zz, 4:5, :]
        for n in range(NC):
            h16[n, 2 * zz : 2 * zz + 2, :] = fr[zz, 2 * n : 2 * n + 2, :]
    tx[x] = jnp.broadcast_to(tot, (8, 128))
    got_t = [send(tx.at[x], tx.at[x], txs.at[d - 1], txr.at[d - 1], at_x(d)) for d in range(1, 4)]
    load_cnt.wait()
    for n in range(NC):
        fan_on(hmat, 0, n, got[n])
    for copy in got_t:
        copy.wait_recv()
    tc[k] = tx[0] + tx[1] + tx[2] + tx[3]
    got_tc = send(tc.at[k], tc.at[k], tcs.at[0], tcr.at[0], at_core)

    got_n = []
    for n in range(NC):
        cols = slice(n * CH, (n + 1) * CH)
        fan_in(got[n])
        h_chunk = hmat[:, :, cols].reshape(128, CH)
        for i in range(8):
            rows = slice(i * 120, (i + 1) * 120)
            modeled = jnp.dot(wp[rows, :], h_chunk, preferred_element_type=F32)
            counts = cnt[rows, cols].astype(F32)
            quo[rows, :] = (counts * pltpu.reciprocal(modeled, approx=True)).astype(BF)
        part = jnp.dot(wt[...], quo[...], preferred_element_type=F32)
        num[n, 0] = part[0:64, :]
        num[n, 1] = part[64:128, :]
        got_n.append(send(num.at[n, 1 - k], numr.at[n], ns.at[n], nr.at[n], at_core))
    got_tc.wait_recv()
    w_totals = tc[0][0:1, :] + tc[1][0:1, :]
    places = iota((16, 128), 0)
    own = (places // 2) * 16 + x * 4 + k * 2 + places % 2 == iota((16, 128), 1)
    w_column = jnp.sum(jnp.where(own, w_totals, 0.0), axis=1, keepdims=True)

    got_bx = []
    for n in range(NC):
        got_n[n].wait_recv()
        both = num[n, k] + numr[n]
        bs[n] = both.reshape(4, 16, CH)
        scale = scale_of(both)
        code = encode(both, scale)
        scale2 = twice(scale)
        for s in range(4):
            bx[n, s, :, 0:CH] = code[16 * s : 16 * s + 16, :]
            bx[n, s, :, CH : CH + 128] = scale2
        got_bx.append([
            send(bx.at[n, (x + d) % 4], bxr.at[n, d - 1], bxs.at[n, d - 1], bxrs.at[n, d - 1], at_x(d))
            for d in range(1, 4)
        ])
    got_bz = []
    for n in range(NC):
        total = bs[n, x]
        for d in (1, 3, 2):
            got_bx[n][d - 1].wait_recv()
            total = total + decode(bxr[n, d - 1, :, 0:CH], bxr[n, d - 1, :, CH : CH + 128])
        scale = scale_of(total)
        code = encode(total, scale)
        scale2 = twice(scale)
        for s in range(8):
            tz[n, s] = total[:, s * ZG : (s + 1) * ZG]
            bz[n, s, :, 0:ZG] = code[:, s * ZG : (s + 1) * ZG]
            bz[n, s, :, ZG : ZG + 128] = scale2
        got_bz.append([
            send(bz.at[n, (z + d) % 8], bzr.at[n, d - 1], bzs.at[n, d - 1], bzrs.at[n, d - 1], at_z(d))
            for d in range(1, 8)
        ])
    got_cz = []
    got_o = []
    for n in range(NC):
        total = tz[n, z]
        for d in range(1, 8):
            got_bz[n][d - 1].wait_recv()
            total = total + decode(bzr[n, d - 1, :, 0:ZG], bzr[n, d - 1, :, ZG : ZG + 128])
        updated = h16[n] * total / w_column
        hu[n] = updated.astype(BF)
        cols = pl.ds(pl.multiple_of(n * CH + z * ZG, ZG), ZG)
        hmat2[slot, :, cols] = hu[n]
        got_cz.append([
            send(hu.at[n], hmat2.at[slot, :, cols], cz.at[n, d - 1], czr.at[n, d - 1], at_z(d))
            for d in range(1, 8)
        ])
        for zz in range(8):
            ho[n, zz] = updated[2 * zz : 2 * zz + 2, :]
    for n in range(NC):
        cols = pl.ds(pl.multiple_of(n * CH + z * ZG, ZG), ZG)
        outr[:, cols] = ho[n, z]
        for d in range(1, 8):
            got_o.append(
                send(ho.at[n, (z + d) % 8], outr.at[:, cols], os_.at[n, d - 1], ors.at[n, d - 1], at_z(d))
            )

    got = []
    for n in range(NC):
        for copy in got_cz[n]:
            copy.wait_recv()
        got.append(fan_out(hmat2, 1, n))
    for n in range(NC):
        fan_on(hmat2, 1, n, got[n])
    for n in range(NC):
        fan_in(got[n])
    h_all = hmat2[...].reshape(128, 2048)
    hn[...] = jnp.dot(pick, h_all, preferred_element_type=F32).astype(BF)
    ht[g] = lax.dot_general(
        jnp.ones((8, 2048), BF), hn[...], (((1,), (1,)), ((), ())), preferred_element_type=F32
    )
    got_h = [
        send(ht.at[g], ht.at[g], hts.at[d - 1], htr.at[d - 1], (c, (g + d) % 8)) for d in range(1, 8)
    ]

    got_y = {}
    for d in (2, 1, 3, 0):
        first_row = ((y + d) % 4) * ROWS
        rows = pl.ds(pl.multiple_of(first_row, 16), ROWS)
        acc = None
        for j in range(4):
            cols = slice(j * 512, (j + 1) * 512)
            modeled = jnp.dot(
                wp[rows, :], hmat2[:, :, cols].reshape(128, 512), preferred_element_type=F32
            )
            counts = cnt[rows, cols].astype(F32)
            quotient = (counts * pltpu.reciprocal(modeled, approx=True)).astype(BF)
            term = lax.dot_general(
                quotient, hn[:, cols], (((1,), (1,)), ((), ())), preferred_element_type=F32
            )
            acc = term if acc is None else acc + term
        if d:
            scale = scale_of(acc)
            dy[d - 1, 0:ROWS, :] = encode(acc, scale)
            dy[d - 1, ROWS : ROWS + 16, :] = twice(scale)
            got_y[d] = send(dy.at[d - 1], dyr.at[d - 1], dys.at[d - 1], dyrs.at[d - 1], at_y(d))
        else:
            wn[...] = acc
    total = wn[...]
    for d in (2, 1, 3):
        got_y[d].wait_recv()
        total = total + decode(dyr[d - 1, 0:ROWS, :], dyr[d - 1, ROWS : ROWS + 16, :])
    scale = scale_of(total)
    dz[0:ROWS, :] = encode(total, scale)
    dz[ROWS : ROWS + 16, :] = twice(scale)
    got_z = send(dz, zr, dzs.at[0], dzr.at[0], at_zh)

    for copy in got_h:
        copy.wait_recv()
    h_totals = ht[0]
    for i in range(1, 8):
        h_totals = h_totals + ht[i]
    for copy in got_o:
        copy.wait_recv()
    h_out[...] = outr[...]

    got_z.wait_recv()
    total = decode(dz[0:ROWS, :], dz[ROWS : ROWS + 16, :]) + decode(zr[0:ROWS, :], zr[ROWS : ROWS + 16, :])
    scale = scale_of(total)
    da[y, 0:ROWS, :] = encode(total, scale)
    da[y, ROWS : ROWS + 16, :] = twice(scale)
    got_w = [send(da.at[y], da.at[y], das.at[d - 1], dar.at[d - 1], at_y(d)) for d in range(1, 4)]
    inverse = spread(1.0 / h_totals, ROWS, 128)
    for d in (0, 1, 3, 2):
        if d:
            got_w[d - 1].wait_recv()
        p = (y + 4 - d) % 4
        rows = pl.ds(pl.multiple_of(p * ROWS, 16), ROWS)
        w_out[rows, :] = wf[rows, :] * (decode(da[p, 0:ROWS, :], da[p, ROWS : ROWS + 16, :]) * inverse)
    for copy in sent:
        copy.wait_send()


def per_device(counts, w_factor, h_factor):
    vmem = pltpu.VMEM
    dma = pltpu.SemaphoreType.DMA
    anywhere = pl.BlockSpec(memory_space=pl.ANY)
    local = pl.BlockSpec(memory_space=pltpu.VMEM)
    return pl.pallas_call(
        kernel,
        out_shape=(
            jax.ShapeDtypeStruct((960, 128), F32),
            jax.ShapeDtypeStruct((2, 2048), F32),
        ),
        in_specs=[anywhere, anywhere, local],
        out_specs=(local, local),
        scratch_shapes=[
            vmem((960, 2048), BF), vmem((960, 128), F32), vmem((960, 128), BF), vmem((128, 960), BF),
            vmem((960, CH), BF),
            vmem((2, 2048), BF), vmem((8, 2, 2048), BF), vmem((16, 2048), F32), vmem((8, 16, 2048), BF),
            vmem((8, 8, 128), F32), vmem((8, 8, 128), F32), vmem((NC, 16, ZG), F32),
            vmem((4, 8, 128), F32), vmem((2, 8, 128), F32),
            vmem((NC, 2, 64, CH), F32), vmem((NC, 64, CH), F32), vmem((NC, 4, 16, CH), F32),
            vmem((NC, 4, 16, CH + 128), BF), vmem((NC, 3, 16, CH + 128), BF),
            vmem((NC, 8, 16, ZG), F32), vmem((NC, 8, 16, ZG + 128), BF), vmem((NC, 7, 16, ZG + 128), BF),
            vmem((NC, 16, ZG), BF), vmem((NC, 8, 2, ZG), F32), vmem((2, 2048), F32),
            vmem((8, 16, 2048), BF), vmem((128, 2048), BF), vmem((8, 8, 128), F32),
            vmem((ROWS, 128), F32), vmem((3, ROWS + 16, 128), BF), vmem((3, ROWS + 16, 128), BF),
            vmem((ROWS + 16, 128), BF), vmem((ROWS + 16, 128), BF), vmem((4, ROWS + 16, 128), BF),
            dma((2,)), dma((7,)), dma((7,)), dma((7,)), dma((7,)), dma((3,)), dma((3,)), dma((1,)), dma((1,)),
            dma((2, NC, 3)), dma((2, NC, 3)), dma((2, NC, 4)), dma((2, NC, 4)), dma((NC,)), dma((NC,)),
            dma((NC, 3)), dma((NC, 3)), dma((NC, 7)), dma((NC, 7)), dma((NC, 7)), dma((NC, 7)),
            dma((NC, 7)), dma((NC, 7)), dma((7,)), dma((7,)),
            dma((3,)), dma((3,)), dma((1,)), dma((1,)), dma((3,)), dma((3,)),
        ],
        compiler_params=pltpu.CompilerParams(
            collective_id=0, has_side_effects=True, vmem_limit_bytes=48 * 1024 * 1024
        ),
        name="nmf_update",
    )(counts, w_factor, h_factor)


def solution(mesh):
    in_specs = (P("cell", "gene"), P("cell", None), P("cell", "gene"))
    out_specs = (P("cell", None), P("cell", "gene"))
    return jax.shard_map(
        per_device, mesh=mesh, in_specs=in_specs, out_specs=out_specs, check_vma=False
    )
```

time: 1280 us -> 88.6 us (0.07)
  the two profiles are of different devices: /device:TPU:116 before, /device:TPU:32 now
where the time goes in v1:
time: 88.6 us; the launch traced here: 88.3 us
  Pallas kernels  82.5 us (93%)
  local copies, waits for them, and re-layouts  5.24 us (6%)
    pallas_call x1, Pallas kernels, per_device(): pl.pallas_call(kernel, out_shape=(jax.ShapeDtypeStruct((960, 128), F32),...  82.5 us
    unnamed x8, local copies, waits for them, and re-layouts  5.24 us

profile of v1, /device:TPU:32, one launch (start us, length us, event | category | flops | bytes accessed | tf_op | source)
XLA Modules:
  0.0 88.3 jit_solution(8633852724823474331)
XLA Ops:
  0.6 0.0 copy-start
  0.6 2.1 %copy-done = bf16[960,2048]{1,0:T(8,128)(2,1)S(1)} copy-done((bf16[960,2048]{1,0:T(8,128)(2,1)S(1)}, bf16[960,2048]{1,0:T(8,128)(2,1)}, u32[]{:S(2)}) %copy-start) | copy-done | bytes 3932184
  2.7 0.0 copy-start.1
  2.7 1.0 %copy-done.1 = f32[960,128]{1,0:T(8,128)S(1)} copy-done((f32[960,128]{1,0:T(8,128)S(1)}, f32[960,128]{1,0:T(8,128)}, u32[]{:S(2)}) %copy-start.1) | copy-done | bytes 491544
  3.8 0.0 copy-start.2
  3.8 0.7 copy-done.2
  4.5 82.5 %nmf_update.1 = (f32[960,128]{1,0:T(8,128)S(1)}, f32[2,2048]{1,0:T(2,128)S(1)}) custom-call(bf16[960,2048]{1,0:T(8,128)(2,1)S(1)} %copy-done, f32[960,128]{1,0:T(8,128)S(1)} %copy-done.1, f32[2,2048]{1,0:T(2,128)S(1)} %copy-done.2), custom_call_target="tpu_custom_call" | custom-call | tf_op jit(solution)/shard_map/nmf_update/pallas_call | solution.py:340
  87.0 0.8 copy.7
  87.7 0.6 copy.8
Async XLA Ops:
  0.6 2.1 %copy-start = (bf16[960,2048]{1,0:T(8,128)(2,1)S(1)}, bf16[960,2048]{1,0:T(8,128)(2,1)}, u32[]{:S(2)}) copy-start(bf16[960,2048]{1,0:T(8,128)(2,1)} %cnt_hbm.1) | copy-start | bytes 11796484
  2.7 1.0 %copy-start.1 = (f32[960,128]{1,0:T(8,128)S(1)}, f32[960,128]{1,0:T(8,128)}, u32[]{:S(2)}) copy-start(f32[960,128]{1,0:T(8,128)} %w_hbm.1) | copy-start | bytes 1474564
  3.8 0.7 copy-start.2

commit v2 on v1

v2 whole, which is shorter than its diff:
```python
import jax
import jax.numpy as jnp
from jax import lax
from jax.experimental import pallas as pl
from jax.experimental.pallas import tpu as pltpu
from jax.sharding import PartitionSpec as P

MESH = pl.DeviceIdType.MESH
BF = jnp.bfloat16
F32 = jnp.float32
NC = 2
CH = 2048 // NC
ZG = CH // 8
ROWS = 240
STARTS, SIZES = (0, 128), (128, 112)
NEAR = (1, 2, 3, 4, 5, 6, 7)
FAR = (7, 6, 5, 4, 3, 2, 1)


def iota(shape, dim):
    return lax.broadcasted_iota(jnp.int32, shape, dim)


def natural(i):
    return ((i % 16) // 2) * 16 + ((i // 16) % 4) * 4 + (i // 64) * 2 + i % 2


def spread(tile, rows, columns):
    wide = jnp.concatenate([tile] * (columns // 128), axis=1) if columns > 128 else tile
    return jnp.concatenate([wide] * (rows // 8), axis=0) if rows > 8 else wide


def scale_of(value):
    rows, columns = value.shape
    top = jnp.full((8, 128), 1e-30, F32)
    for r in range(0, rows, 8):
        for c in range(0, columns, 128):
            top = jnp.maximum(top, value[r : r + 8, c : c + 128])
    return top.astype(BF)


def encode(value, scale):
    rows, columns = value.shape
    share = value * spread(32768.0 / scale.astype(F32), rows, columns)
    square = share * share
    fourth = square * square
    return (fourth * fourth).astype(BF)


def decode(code, scale16):
    rows, columns = code.shape
    unit = scale16[0:8, :].astype(F32) * (1.0 / 32768.0)
    root = jnp.sqrt(jnp.sqrt(jnp.sqrt(code.astype(F32))))
    return root * spread(unit, rows, columns)


def twice(scale):
    wide = scale.astype(F32)
    return jnp.concatenate([wide, wide], axis=0).astype(BF)


def kernel(
    cnt_hbm, w_hbm, h_hbm, w_out, h_out,
    cnt, wf, h_in, wp, wt, quo,
    hown, ha, hx32, hmat, fm, fr, h16, tx, tc,
    num, numr, bs, bx, bxr, tz, bz, bzr, hu, ho, outr, hmat2, hn, ht, hz,
    wn, dy, dyr, dz, zr, da,
    ls, as_, ar, fs, frs, txs, txr, tcs, tcr,
    xs, xr, cs, cr, ns, nr, bxs, bxrs, bzs, bzrs, cz, czr, os_, ors, hts, htr, hzs, hzr,
    dys, dyrs, dzs, dzr, das, dar,
):
    c = lax.axis_index("cell")
    g = lax.axis_index("gene")
    z, x, k = c // 8, (c // 2) % 4, c % 2
    y, zh = g // 2, g % 2
    slot = k * 4 + x

    turn = jnp.where(z < 4, 1, 7)

    def z_of(d):
        return (z + turn * d) % 8

    def at_z(d):
        return (z_of(d) * 8 + x * 2 + k, g)

    def at_x(d):
        return (z * 8 + ((x + d) % 4) * 2 + k, g)

    def at_y(d):
        return (c, ((y + d) % 4) * 2 + zh)

    def genes(n, owner):
        return pl.ds(pl.multiple_of(n * CH + owner * ZG, ZG), ZG)

    at_core = (z * 8 + x * 2 + (1 - k), g)
    at_zh = (c, y * 2 + (1 - zh))
    sent = []

    def remote(src, dst, ssem, rsem, device):
        return pltpu.make_async_remote_copy(
            src_ref=src, dst_ref=dst, send_sem=ssem, recv_sem=rsem, device_id=device, device_id_type=MESH
        )

    def due(copy):
        return copy

    def send(src, dst, ssem, rsem, device):
        copy = remote(src, dst, ssem, rsem, device)
        copy.start()
        sent.append(copy)
        return due(copy)

    def send_z(src, dst, ssem, rsem):
        for d in FAR:
            copy = remote(src(z_of(d)), dst(z), ssem.at[d], rsem.at[z], at_z(d))
            copy.start()
            sent.append(copy)
        return [
            due(remote(src(z_of(d)), dst(z_of(d)), ssem.at[d], rsem.at[z_of(d)], at_z(d))) for d in NEAR
        ]

    barrier = pltpu.get_barrier_semaphore()
    friends = [at_z(d) for d in FAR] + [at_x(d) for d in range(1, 4)] + [at_core]
    friends += [at_y(d) for d in range(1, 4)] + [at_zh]
    for friend in friends:
        pl.semaphore_signal(barrier, inc=1, device_id=friend, device_id_type=MESH)

    load_h = pltpu.make_async_copy(h_hbm, h_in, ls.at[2])
    load_w = pltpu.make_async_copy(w_hbm, wf, ls.at[1])
    load_cnt = pltpu.make_async_copy(cnt_hbm, cnt, ls.at[0])
    load_h.start()
    load_w.start()
    load_cnt.start()
    load_h.wait()
    hown[...] = h_in[...].astype(BF)
    pl.semaphore_wait(barrier, len(friends))

    got_a = send_z(lambda s: hown, lambda s: ha.at[s], as_, ar)
    ha[z] = hown[...]

    load_w.wait()
    w_all = wf[...]
    w_sum = jnp.sum(w_all, axis=0, keepdims=True)
    h_own = h_in[...]
    for zz in range(8):
        for n in range(NC):
            base = n * CH + zz * ZG
            fm[zz, 2 * n : 2 * n + 2, :] = h_own[:, base : base + ZG]
        fm[zz, 4:5, :] = w_sum
    got_f = send_z(lambda s: fm.at[s], lambda s: fr.at[s], fs, frs)
    fr[z] = fm[z]
    w_copy = w_all.astype(BF)
    pick = (iota((128, 128), 0) == natural(iota((128, 128), 1))).astype(F32).astype(BF)
    pick_t = (natural(iota((128, 128), 0)) == iota((128, 128), 1)).astype(F32).astype(BF)
    wp[...] = jnp.dot(w_copy, pick, preferred_element_type=F32).astype(BF)
    wt[...] = lax.dot_general(
        pick_t, w_copy, (((1,), (1,)), ((), ())), preferred_element_type=F32
    ).astype(BF)

    for copy in got_a:
        copy.wait_recv()
    for zz in range(8):
        hx32[2 * zz : 2 * zz + 2, :] = ha[zz].astype(F32)
    hmat[slot] = hx32[...].astype(BF)

    def fan_out(buf, phase, n):
        cols = pl.ds(n * CH, CH)
        mine = buf.at[slot, :, cols]
        got_x = {d: send(mine, mine, xs.at[phase, n, d - 1], xr.at[phase, n, d - 1], at_x(d)) for d in (2, 1, 3)}
        got_c = [send(mine, mine, cs.at[phase, n, 0], cr.at[phase, n, 0], at_core)]
        return got_x, got_c

    def fan_on(buf, phase, n, got):
        cols = pl.ds(n * CH, CH)
        for d in (1, 3, 2):
            got[0][d].wait_recv()
            piece = buf.at[k * 4 + (x + 4 - d) % 4, :, cols]
            got[1].append(send(piece, piece, cs.at[phase, n, d], cr.at[phase, n, d], at_core))

    def fan_in(got):
        for copy in got[1]:
            copy.wait_recv()

    def quotients(n, first, last):
        cols = slice(n * CH, (n + 1) * CH)
        h_chunk = hmat[:, :, cols].reshape(128, CH)
        for i in range(first, last):
            rows = slice(i * 120, (i + 1) * 120)
            modeled = jnp.dot(wp[rows, :], h_chunk, preferred_element_type=F32)
            counts = cnt[rows, cols].astype(F32)
            quo[rows, :] = (counts * pltpu.reciprocal(modeled, approx=True)).astype(BF)

    def numerator(n):
        part = jnp.dot(wt[...], quo[...], preferred_element_type=F32)
        num[n, 0] = part[0:64, :]
        num[n, 1] = part[64:128, :]
        return send(num.at[n, 1 - k], numr.at[n], ns.at[n], nr.at[n], at_core)

    def sum_core(n, got):
        got.wait_recv()
        both = num[n, k] + numr[n]
        bs[n] = both.reshape(4, 16, CH)
        scale = scale_of(both)
        code = encode(both, scale)
        scale2 = twice(scale)
        for s in range(4):
            bx[n, s, :, 0:CH] = code[16 * s : 16 * s + 16, :]
            bx[n, s, :, CH : CH + 128] = scale2
        return {
            d: send(bx.at[n, (x + d) % 4], bxr.at[n, d - 1], bxs.at[n, d - 1], bxrs.at[n, d - 1], at_x(d))
            for d in (2, 1, 3)
        }

    def sum_x(n, got):
        total = bs[n, x]
        for d in (1, 3, 2):
            got[d].wait_recv()
            total = total + decode(bxr[n, d - 1, :, 0:CH], bxr[n, d - 1, :, CH : CH + 128])
        scale = scale_of(total)
        code = encode(total, scale)
        scale2 = twice(scale)
        for s in range(8):
            tz[n, s] = total[:, s * ZG : (s + 1) * ZG]
            bz[n, s, :, 0:ZG] = code[:, s * ZG : (s + 1) * ZG]
            bz[n, s, :, ZG : ZG + 128] = scale2
        return send_z(lambda s: bz.at[n, s], lambda s: bzr.at[n, s], bzs.at[n], bzrs.at[n])

    def sum_z(n, got):
        total = tz[n, z]
        for d in NEAR:
            s = z_of(d)
            got[d - 1].wait_recv()
            total = total + decode(bzr[n, s, :, 0:ZG], bzr[n, s, :, ZG : ZG + 128])
        updated = h16[n] * total / w_column
        hu[n] = updated.astype(BF)
        hmat2[slot, :, genes(n, z)] = hu[n]
        copies = send_z(lambda s: hu.at[n], lambda s: hmat2.at[slot, :, genes(n, s)], cz.at[n], czr.at[n])
        for zz in range(8):
            ho[n, zz] = updated[2 * zz : 2 * zz + 2, :]
        return copies

    got = [fan_out(hmat, 0, n) for n in range(NC)]

    for copy in got_f:
        copy.wait_recv()
    tot = jnp.zeros((1, 128), F32)
    for zz in range(8):
        tot = tot + fr[zz, 4:5, :]
        for n in range(NC):
            h16[n, 2 * zz : 2 * zz + 2, :] = fr[zz, 2 * n : 2 * n + 2, :]
    tx[x] = jnp.broadcast_to(tot, (8, 128))
    got_t = [send(tx.at[x], tx.at[x], txs.at[d - 1], txr.at[d - 1], at_x(d)) for d in (2, 1, 3)]
    load_cnt.wait()

    fan_on(hmat, 0, 0, got[0])
    fan_in(got[0])
    quotients(0, 0, 4)
    fan_on(hmat, 0, 1, got[1])
    quotients(0, 4, 8)
    got_n = [numerator(0)]
    fan_in(got[1])
    quotients(1, 0, 4)
    got_bx = [sum_core(0, got_n[0])]
    quotients(1, 4, 8)
    got_n.append(numerator(1))
    for copy in got_t:
        copy.wait_recv()
    tc[k] = tx[0] + tx[1] + tx[2] + tx[3]
    got_tc = send(tc.at[k], tc.at[k], tcs.at[0], tcr.at[0], at_core)
    got_bz = [sum_x(0, got_bx[0])]
    got_bx.append(sum_core(1, got_n[1]))
    got_tc.wait_recv()
    w_totals = tc[0][0:1, :] + tc[1][0:1, :]
    places = iota((16, 128), 0)
    own = (places // 2) * 16 + x * 4 + k * 2 + places % 2 == iota((16, 128), 1)
    w_column = jnp.sum(jnp.where(own, w_totals, 0.0), axis=1, keepdims=True)
    got_bz.append(sum_x(1, got_bx[1]))
    got_cz = [sum_z(n, got_bz[n]) for n in range(NC)]

    got = []
    for n in range(NC):
        for copy in got_cz[n]:
            copy.wait_recv()
        got.append(fan_out(hmat2, 1, n))
    got_o = []
    for n in range(NC):
        outr[:, genes(n, z)] = ho[n, z]
        got_o += send_z(lambda s: ho.at[n, s], lambda s: outr.at[:, genes(n, s)], os_.at[n], ors.at[n])

    fan_on(hmat2, 1, 0, got[0])
    fan_in(got[0])

    def h_natural(n):
        cols = slice(n * CH, (n + 1) * CH)
        hn[:, cols] = jnp.dot(
            pick, hmat2[:, :, cols].reshape(128, CH), preferred_element_type=F32
        ).astype(BF)

    def w_part(n, rows):
        acc = None
        for j in range(n * CH // 512, (n + 1) * CH // 512):
            cols = slice(j * 512, (j + 1) * 512)
            modeled = jnp.dot(
                wp[rows, :], hmat2[:, :, cols].reshape(128, 512), preferred_element_type=F32
            )
            counts = cnt[rows, cols].astype(F32)
            quotient = (counts * pltpu.reciprocal(modeled, approx=True)).astype(BF)
            term = lax.dot_general(
                quotient, hn[:, cols], (((1,), (1,)), ((), ())), preferred_element_type=F32
            )
            acc = term if acc is None else acc + term
        return acc

    h_natural(0)
    for i in range(2):
        rows = slice(i * 240, (i + 1) * 240)
        wn[rows, :] = w_part(0, rows)
    fan_on(hmat2, 1, 1, got[1])
    for i in range(2, 4):
        rows = slice(i * 240, (i + 1) * 240)
        wn[rows, :] = w_part(0, rows)
    fan_in(got[1])
    h_natural(1)

    def code_y(part, d, value):
        size = SIZES[part]
        scale = scale_of(value)
        dy[part, d - 1, 0:size, :] = encode(value, scale)
        dy[part, d - 1, size : size + 16, :] = twice(scale)
        whole = pl.ds(0, size + 16)
        return send(
            dy.at[part, d - 1, whole], dyr.at[part, d - 1, whole], dys.at[part, d - 1], dyrs.at[part, d - 1], at_y(d)
        )

    def rows_of(part, owner):
        return pl.ds(pl.multiple_of(owner * ROWS + STARTS[part], 16), SIZES[part])

    def sum_y(part, got):
        size = SIZES[part]
        total = wn[rows_of(part, y), :]
        for d in (1, 3, 2):
            got[d].wait_recv()
            total = total + decode(dyr[part, d - 1, 0:size, :], dyr[part, d - 1, size : size + 16, :])
        scale = scale_of(total)
        dz[part, 0:size, :] = encode(total, scale)
        dz[part, size : size + 16, :] = twice(scale)
        whole = pl.ds(0, size + 16)
        return send(dz.at[part, whole], zr.at[part, whole], dzs.at[part], dzr.at[part], at_zh)

    got_y = [{}, {}]
    got_z = []
    for part in range(2):
        for d in (2, 1, 3, 0):
            rows = rows_of(part, (y + d) % 4)
            value = wn[rows, :] + w_part(1, rows)
            if d:
                got_y[part][d] = code_y(part, d, value)
            else:
                wn[rows, :] = value
            if part == 1 and d == 1:
                got_z.append(sum_y(0, got_y[0]))
    ht[y] = lax.dot_general(
        jnp.ones((8, 2048), BF), hn[...], (((1,), (1,)), ((), ())), preferred_element_type=F32
    )
    got_h = [send(ht.at[y], ht.at[y], hts.at[d - 1], htr.at[d - 1], at_y(d)) for d in (2, 1, 3)]
    got_z.append(sum_y(1, got_y[1]))
    for copy in got_h:
        copy.wait_recv()
    hz[zh] = ht[0] + ht[1] + ht[2] + ht[3]
    got_hz = send(hz.at[zh], hz.at[zh], hzs.at[0], hzr.at[0], at_zh)
    for copy in got_o:
        copy.wait_recv()
    h_out[...] = outr[...]

    got_w = []
    for part in range(2):
        size = SIZES[part]
        got_z[part].wait_recv()
        total = decode(dz[part, 0:size, :], dz[part, size : size + 16, :])
        total = total + decode(zr[part, 0:size, :], zr[part, size : size + 16, :])
        scale = scale_of(total)
        da[part, y, 0:size, :] = encode(total, scale)
        da[part, y, size : size + 16, :] = twice(scale)
        mine = da.at[part, y, pl.ds(0, size + 16)]
        got_w.append({d: send(mine, mine, das.at[part, d - 1], dar.at[part, d - 1], at_y(d)) for d in (2, 1, 3)})
    got_hz.wait_recv()
    h_totals = hz[0] + hz[1]
    for part in range(2):
        size = SIZES[part]
        inverse = spread(1.0 / h_totals, size, 128)
        for d in (0, 1, 3, 2):
            if d:
                got_w[part][d].wait_recv()
            p = (y + 4 - d) % 4
            rows = rows_of(part, p)
            share = decode(da[part, p, 0:size, :], da[part, p, size : size + 16, :])
            w_out[rows, :] = wf[rows, :] * (share * inverse)
    for copy in sent:
        copy.wait_send()


def per_device(counts, w_factor, h_factor):
    vmem = pltpu.VMEM
    dma = pltpu.SemaphoreType.DMA
    far = pl.BlockSpec(memory_space=pl.ANY)
    local = pl.BlockSpec(memory_space=pltpu.VMEM)
    return pl.pallas_call(
        kernel,
        out_shape=(
            jax.ShapeDtypeStruct((960, 128), F32),
            jax.ShapeDtypeStruct((2, 2048), F32),
        ),
        in_specs=[far, far, far],
        out_specs=(local, local),
        scratch_shapes=[
            vmem((960, 2048), BF), vmem((960, 128), F32), vmem((2, 2048), F32), vmem((960, 128), BF), vmem((128, 960), BF),
            vmem((960, CH), BF),
            vmem((2, 2048), BF), vmem((8, 2, 2048), BF), vmem((16, 2048), F32), vmem((8, 16, 2048), BF),
            vmem((8, 8, 128), F32), vmem((8, 8, 128), F32), vmem((NC, 16, ZG), F32),
            vmem((4, 8, 128), F32), vmem((2, 8, 128), F32),
            vmem((NC, 2, 64, CH), F32), vmem((NC, 64, CH), F32), vmem((NC, 4, 16, CH), F32),
            vmem((NC, 4, 16, CH + 128), BF), vmem((NC, 3, 16, CH + 128), BF),
            vmem((NC, 8, 16, ZG), F32), vmem((NC, 8, 16, ZG + 128), BF), vmem((NC, 8, 16, ZG + 128), BF),
            vmem((NC, 16, ZG), BF), vmem((NC, 8, 2, ZG), F32), vmem((2, 2048), F32),
            vmem((8, 16, 2048), BF), vmem((128, 2048), BF), vmem((4, 8, 128), F32), vmem((2, 8, 128), F32),
            vmem((960, 128), F32), vmem((2, 3, 144, 128), BF), vmem((2, 3, 144, 128), BF),
            vmem((2, 144, 128), BF), vmem((2, 144, 128), BF), vmem((2, 4, 144, 128), BF),
            dma((3,)), dma((8,)), dma((8,)), dma((8,)), dma((8,)), dma((3,)), dma((3,)), dma((1,)), dma((1,)),
            dma((2, NC, 3)), dma((2, NC, 3)), dma((2, NC, 4)), dma((2, NC, 4)), dma((NC,)), dma((NC,)),
            dma((NC, 3)), dma((NC, 3)), dma((NC, 8)), dma((NC, 8)), dma((NC, 8)), dma((NC, 8)),
            dma((NC, 8)), dma((NC, 8)), dma((3,)), dma((3,)), dma((1,)), dma((1,)),
            dma((2, 3)), dma((2, 3)), dma((2,)), dma((2,)), dma((2, 3)), dma((2, 3)),
        ],
        compiler_params=pltpu.CompilerParams(
            collective_id=0, has_side_effects=True, vmem_limit_bytes=60 * 1024 * 1024
        ),
        name="nmf_update",
    )(counts, w_factor, h_factor)


def solution(mesh):
    in_specs = (P("cell", "gene"), P("cell", None), P("cell", "gene"))
    out_specs = (P("cell", None), P("cell", "gene"))
    return jax.shard_map(
        per_device, mesh=mesh, in_specs=in_specs, out_specs=out_specs, check_vma=False
    )
```

time: 88.6 us -> 81.8 us (0.923)
  the two profiles are of different devices: /device:TPU:32 before, /device:TPU:2 now
where the time goes in v2:
time: 81.8 us; the launch traced here: 81.5 us
  Pallas kernels  77.7 us (95%)
  local copies, waits for them, and re-layouts  3.16 us (4%)
    pallas_call x1, Pallas kernels, per_device(): pl.pallas_call(kernel, out_shape=(jax.ShapeDtypeStruct((960, 128), F32),...  77.7 us
    unnamed x2, local copies, waits for them, and re-layouts  3.16 us

profile of v2, /device:TPU:2, one launch (start us, length us, event | category | flops | bytes accessed | tf_op | source)
XLA Modules:
  0.0 81.5 jit_solution(3674976615795877767)
XLA Ops:
  0.6 77.7 %nmf_update.1 = (f32[960,128]{1,0:T(8,128)}, f32[2,2048]{1,0:T(2,128)}) custom-call(bf16[960,2048]{1,0:T(8,128)(2,1)} %cnt_hbm.1, f32[960,128]{1,0:T(8,128)} %w_hbm.1, f32[2,2048]{1,0:T(2,128)} %h_hbm.1), custom_call_target="tpu_custom_call" | custom-call | tf_op jit(solution)/shard_map/nmf_update/pallas_call | solution.py:407
  78.3 1.8 %copy.7 = f32[960,128]{1,0:T(8,128)} copy(f32[960,128]{1,0:T(8,128)} %get-tuple-element.4) | data formatting | bytes 983040
  80.2 1.3 %copy.8 = f32[2,2048]{1,0:T(2,128)} copy(f32[2,2048]{1,0:T(2,128)} %get-tuple-element.5) | data formatting | bytes 32768

commit v3 on v2

--- a/solution.py
+++ b/solution.py
@@ -11,6 +11,7 @@
 NC = 2
 CH = 2048 // NC
 ZG = CH // 8
+HALF = CH // 2
 ROWS = 240
 STARTS, SIZES = (0, 128), (128, 112)
 NEAR = (1, 2, 3, 4, 5, 6, 7)
@@ -64,10 +65,10 @@
     cnt, wf, h_in, wp, wt, quo,
     hown, ha, hx32, hmat, fm, fr, h16, tx, tc,
     num, numr, bs, bx, bxr, tz, bz, bzr, hu, ho, outr, hmat2, hn, ht, hz,
-    wn, dy, dyr, dz, zr, da,
+    wn, dy, dyr, dz, zr, da, wv,
     ls, as_, ar, fs, frs, txs, txr, tcs, tcr,
     xs, xr, cs, cr, ns, nr, bxs, bxrs, bzs, bzrs, cz, czr, os_, ors, hts, htr, hzs, hzr,
-    dys, dyrs, dzs, dzr, das, dar,
+    dys, dyrs, dzs, dzr, das, dar, gs,
 ):
     c = lax.axis_index("cell")
     g = lax.axis_index("gene")
@@ -75,10 +76,10 @@
     y, zh = g // 2, g % 2
     slot = k * 4 + x
 
-    turn = jnp.where(z < 4, 1, 7)
+    half = z // 4
 
     def z_of(d):
-        return (z + turn * d) % 8
+        return half * 4 + (z + d) % 4 if d < 4 else half * (7 - d) + (1 - half) * d
 
     def at_z(d):
         return (z_of(d) * 8 + x * 2 + k, g)
@@ -157,21 +158,21 @@
         pick_t, w_copy, (((1,), (1,)), ((), ())), preferred_element_type=F32
     ).astype(BF)
 
-    for copy in got_a:
-        copy.wait_recv()
-    for zz in range(8):
-        hx32[2 * zz : 2 * zz + 2, :] = ha[zz].astype(F32)
-    hmat[slot] = hx32[...].astype(BF)
-
-    def fan_out(buf, phase, n):
-        cols = pl.ds(n * CH, CH)
+    for far, copies in ((0, got_a[0:3]), (1, got_a[3:7])):
+        for copy in copies:
+            copy.wait_recv()
+        at = half * (1 - far) + (1 - half) * far
+        for j in range(4):
+            hx32[at, 2 * j : 2 * j + 2, :] = ha[at * 4 + j].astype(F32)
+    hmat[slot] = hx32[...].reshape(16, 2048).astype(BF)
+
+    def fan_out(buf, phase, n, cols):
         mine = buf.at[slot, :, cols]
         got_x = {d: send(mine, mine, xs.at[phase, n, d - 1], xr.at[phase, n, d - 1], at_x(d)) for d in (2, 1, 3)}
         got_c = [send(mine, mine, cs.at[phase, n, 0], cr.at[phase, n, 0], at_core)]
         return got_x, got_c
 
-    def fan_on(buf, phase, n, got):
-        cols = pl.ds(n * CH, CH)
+    def fan_on(buf, phase, n, cols, got):
         for d in (1, 3, 2):
             got[0][d].wait_recv()
             piece = buf.at[k * 4 + (x + 4 - d) % 4, :, cols]
@@ -239,7 +240,7 @@
             ho[n, zz] = updated[2 * zz : 2 * zz + 2, :]
         return copies
 
-    got = [fan_out(hmat, 0, n) for n in range(NC)]
+    got = [fan_out(hmat, 0, n, pl.ds(n * CH, CH)) for n in range(NC)]
 
     for copy in got_f:
         copy.wait_recv()
@@ -252,10 +253,10 @@
     got_t = [send(tx.at[x], tx.at[x], txs.at[d - 1], txr.at[d - 1], at_x(d)) for d in (2, 1, 3)]
     load_cnt.wait()
 
-    fan_on(hmat, 0, 0, got[0])
+    fan_on(hmat, 0, 0, pl.ds(0, CH), got[0])
     fan_in(got[0])
     quotients(0, 0, 4)
-    fan_on(hmat, 0, 1, got[1])
+    fan_on(hmat, 0, 1, pl.ds(CH, CH), got[1])
     quotients(0, 4, 8)
     got_n = [numerator(0)]
     fan_in(got[1])
@@ -277,31 +278,45 @@
     got_bz.append(sum_x(1, got_bx[1]))
     got_cz = [sum_z(n, got_bz[n]) for n in range(NC)]
 
+    def columns(piece):
+        at = half if piece < 2 else 1 - half
+        return pl.ds(pl.multiple_of((piece % 2) * CH + at * HALF, HALF), HALF)
+
     got = []
-    for n in range(NC):
-        for copy in got_cz[n]:
+
+    def z_then_out(piece):
+        for copy in got_cz[piece % 2][0:3] if piece < 2 else got_cz[piece % 2][3:7]:
             copy.wait_recv()
-        got.append(fan_out(hmat2, 1, n))
+        got.append(fan_out(hmat2, 1, piece, columns(piece)))
+
+    def pass_on(piece):
+        fan_on(hmat2, 1, piece, columns(piece), got[piece])
+
+    z_then_out(0)
+    z_then_out(1)
+    z_then_out(2)
+    pass_on(0)
+    z_then_out(3)
+    pass_on(1)
     got_o = []
     for n in range(NC):
         outr[:, genes(n, z)] = ho[n, z]
         got_o += send_z(lambda s: ho.at[n, s], lambda s: outr.at[:, genes(n, s)], os_.at[n], ors.at[n])
-
-    fan_on(hmat2, 1, 0, got[0])
     fan_in(got[0])
-
-    def h_natural(n):
-        cols = slice(n * CH, (n + 1) * CH)
+    fan_in(got[1])
+
+    def h_natural(piece):
+        cols = columns(piece)
         hn[:, cols] = jnp.dot(
-            pick, hmat2[:, :, cols].reshape(128, CH), preferred_element_type=F32
+            pick, hmat2[:, :, cols].reshape(128, HALF), preferred_element_type=F32
         ).astype(BF)
 
-    def w_part(n, rows):
+    def w_part(far, rows):
         acc = None
-        for j in range(n * CH // 512, (n + 1) * CH // 512):
-            cols = slice(j * 512, (j + 1) * 512)
+        for piece in (2 * far, 2 * far + 1):
+            cols = columns(piece)
             modeled = jnp.dot(
-                wp[rows, :], hmat2[:, :, cols].reshape(128, 512), preferred_element_type=F32
+                wp[rows, :], hmat2[:, :, cols].reshape(128, HALF), preferred_element_type=F32
             )
             counts = cnt[rows, cols].astype(F32)
             quotient = (counts * pltpu.reciprocal(modeled, approx=True)).astype(BF)
@@ -312,15 +327,17 @@
         return acc
 
     h_natural(0)
-    for i in range(2):
+    h_natural(1)
+    for i in range(4):
         rows = slice(i * 240, (i + 1) * 240)
         wn[rows, :] = w_part(0, rows)
-    fan_on(hmat2, 1, 1, got[1])
-    for i in range(2, 4):
-        rows = slice(i * 240, (i + 1) * 240)
-        wn[rows, :] = w_part(0, rows)
-    fan_in(got[1])
-    h_natural(1)
+        if i == 1:
+            pass_on(2)
+    pass_on(3)
+    fan_in(got[2])
+    fan_in(got[3])
+    h_natural(2)
+    h_natural(3)
 
     def code_y(part, d, value):
         size = SIZES[part]
@@ -370,7 +387,8 @@
     got_hz = send(hz.at[zh], hz.at[zh], hzs.at[0], hzr.at[0], at_zh)
     for copy in got_o:
         copy.wait_recv()
-    h_out[...] = outr[...]
+    give_h = pltpu.make_async_copy(outr, h_out, ls.at[2])
+    give_h.start()
 
     got_w = []
     for part in range(2):
@@ -385,6 +403,7 @@
         got_w.append({d: send(mine, mine, das.at[part, d - 1], dar.at[part, d - 1], at_y(d)) for d in (2, 1, 3)})
     got_hz.wait_recv()
     h_totals = hz[0] + hz[1]
+    gives = [give_h]
     for part in range(2):
         size = SIZES[part]
         inverse = spread(1.0 / h_totals, size, 128)
@@ -394,28 +413,41 @@
             p = (y + 4 - d) % 4
             rows = rows_of(part, p)
             share = decode(da[part, p, 0:size, :], da[part, p, size : size + 16, :])
-            w_out[rows, :] = wf[rows, :] * (share * inverse)
+            wv[rows, :] = wf[rows, :] * (share * inverse)
+            given = pltpu.make_async_copy(wv.at[rows, :], w_out.at[rows, :], gs.at[part, d])
+            given.start()
+            gives.append(given)
     for copy in sent:
         copy.wait_send()
+    for given in gives:
+        given.wait()
+
+
+def hand_on(w_in, h_in, w_out, h_out, sems):
+    copies = [pltpu.make_async_copy(h_in, h_out, sems.at[4])]
+    for i in range(4):
+        rows = pl.ds(i * ROWS, ROWS)
+        copies.append(pltpu.make_async_copy(w_in.at[rows, :], w_out.at[rows, :], sems.at[i]))
+    for copy in copies:
+        copy.start()
+    for copy in copies:
+        copy.wait()
 
 
 def per_device(counts, w_factor, h_factor):
     vmem = pltpu.VMEM
     dma = pltpu.SemaphoreType.DMA
     far = pl.BlockSpec(memory_space=pl.ANY)
-    local = pl.BlockSpec(memory_space=pltpu.VMEM)
-    return pl.pallas_call(
+    shapes = (jax.ShapeDtypeStruct((960, 128), F32), jax.ShapeDtypeStruct((2, 2048), F32))
+    results = pl.pallas_call(
         kernel,
-        out_shape=(
-            jax.ShapeDtypeStruct((960, 128), F32),
-            jax.ShapeDtypeStruct((2, 2048), F32),
-        ),
+        out_shape=shapes,
         in_specs=[far, far, far],
-        out_specs=(local, local),
+        out_specs=(far, far),
         scratch_shapes=[
             vmem((960, 2048), BF), vmem((960, 128), F32), vmem((2, 2048), F32), vmem((960, 128), BF), vmem((128, 960), BF),
             vmem((960, CH), BF),
-            vmem((2, 2048), BF), vmem((8, 2, 2048), BF), vmem((16, 2048), F32), vmem((8, 16, 2048), BF),
+            vmem((2, 2048), BF), vmem((8, 2, 2048), BF), vmem((2, 8, 2048), F32), vmem((8, 16, 2048), BF),
             vmem((8, 8, 128), F32), vmem((8, 8, 128), F32), vmem((NC, 16, ZG), F32),
             vmem((4, 8, 128), F32), vmem((2, 8, 128), F32),
             vmem((NC, 2, 64, CH), F32), vmem((NC, 64, CH), F32), vmem((NC, 4, 16, CH), F32),
@@ -424,18 +456,26 @@
             vmem((NC, 16, ZG), BF), vmem((NC, 8, 2, ZG), F32), vmem((2, 2048), F32),
             vmem((8, 16, 2048), BF), vmem((128, 2048), BF), vmem((4, 8, 128), F32), vmem((2, 8, 128), F32),
             vmem((960, 128), F32), vmem((2, 3, 144, 128), BF), vmem((2, 3, 144, 128), BF),
-            vmem((2, 144, 128), BF), vmem((2, 144, 128), BF), vmem((2, 4, 144, 128), BF),
+            vmem((2, 144, 128), BF), vmem((2, 144, 128), BF), vmem((2, 4, 144, 128), BF), vmem((960, 128), F32),
             dma((3,)), dma((8,)), dma((8,)), dma((8,)), dma((8,)), dma((3,)), dma((3,)), dma((1,)), dma((1,)),
-            dma((2, NC, 3)), dma((2, NC, 3)), dma((2, NC, 4)), dma((2, NC, 4)), dma((NC,)), dma((NC,)),
+            dma((2, 4, 3)), dma((2, 4, 3)), dma((2, 4, 4)), dma((2, 4, 4)), dma((NC,)), dma((NC,)),
             dma((NC, 3)), dma((NC, 3)), dma((NC, 8)), dma((NC, 8)), dma((NC, 8)), dma((NC, 8)),
             dma((NC, 8)), dma((NC, 8)), dma((3,)), dma((3,)), dma((1,)), dma((1,)),
-            dma((2, 3)), dma((2, 3)), dma((2,)), dma((2,)), dma((2, 3)), dma((2, 3)),
+            dma((2, 3)), dma((2, 3)), dma((2,)), dma((2,)), dma((2, 3)), dma((2, 3)), dma((2, 4)),
         ],
         compiler_params=pltpu.CompilerParams(
             collective_id=0, has_side_effects=True, vmem_limit_bytes=60 * 1024 * 1024
         ),
         name="nmf_update",
     )(counts, w_factor, h_factor)
+    return pl.pallas_call(
+        hand_on,
+        out_shape=shapes,
+        in_specs=[far, far],
+        out_specs=(far, far),
+        scratch_shapes=[dma((5,))],
+        name="hand_on",
+    )(*results)
 
 
 def solution(mesh):

time: 81.8 us -> 94.2 us (1.15)
  the two profiles are of different devices: /device:TPU:2 before, /device:TPU:8 now
where the time goes in v3:
time: 94.2 us; the launch traced here: 94 us
  Pallas kernels  93.4 us (99%)
    pallas_call x1, Pallas kernels, per_device(): pl.pallas_call(kernel, out_shape=shapes, in_specs=[far, far, far], out_sp...  76.9 us
    pallas_call x1, Pallas kernels, per_device(): pl.pallas_call(hand_on, out_shape=shapes, in_specs=[far, far], out_specs=...  16.5 us

profile of v3, /device:TPU:8, one launch (start us, length us, event | category | flops | bytes accessed | tf_op | source)
XLA Modules:
  0.0 94.0 jit_solution(13637837122707524684)
XLA Ops:
  0.6 76.9 %nmf_update.1 = (f32[960,128]{1,0:T(8,128)}, f32[2,2048]{1,0:T(2,128)}) custom-call(bf16[960,2048]{1,0:T(8,128)(2,1)} %cnt_hbm.1, f32[960,128]{1,0:T(8,128)} %w_hbm.1, f32[2,2048]{1,0:T(2,128)} %h_hbm.1), custom_call_target="tpu_custom_call" | custom-call | tf_op jit(solution)/shard_map/nmf_update/pallas_call | solution.py:442
  77.5 16.5 %hand_on.1 = (f32[960,128]{1,0:T(8,128)}, f32[2,2048]{1,0:T(2,128)}) custom-call(f32[960,128]{1,0:T(8,128)} %get-tuple-element.4.w_in, f32[2,2048]{1,0:T(2,128)} %get-tuple-element.5.h_in), custom_call_target="tpu_custom_call" | custom-call | tf_op jit(solution)/shard_map/hand_on/pallas_call | solution.py:471

commit v4 on v3

--- a/solution.py
+++ b/solution.py
@@ -254,28 +254,24 @@
     load_cnt.wait()
 
     fan_on(hmat, 0, 0, pl.ds(0, CH), got[0])
-    fan_in(got[0])
-    quotients(0, 0, 4)
     fan_on(hmat, 0, 1, pl.ds(CH, CH), got[1])
-    quotients(0, 4, 8)
-    got_n = [numerator(0)]
-    fan_in(got[1])
-    quotients(1, 0, 4)
+    got_n = []
+    for n in range(NC):
+        fan_in(got[n])
+        quotients(n, 0, 8)
+        got_n.append(numerator(n))
     got_bx = [sum_core(0, got_n[0])]
-    quotients(1, 4, 8)
-    got_n.append(numerator(1))
     for copy in got_t:
         copy.wait_recv()
     tc[k] = tx[0] + tx[1] + tx[2] + tx[3]
     got_tc = send(tc.at[k], tc.at[k], tcs.at[0], tcr.at[0], at_core)
-    got_bz = [sum_x(0, got_bx[0])]
     got_bx.append(sum_core(1, got_n[1]))
     got_tc.wait_recv()
     w_totals = tc[0][0:1, :] + tc[1][0:1, :]
     places = iota((16, 128), 0)
     own = (places // 2) * 16 + x * 4 + k * 2 + places % 2 == iota((16, 128), 1)
     w_column = jnp.sum(jnp.where(own, w_totals, 0.0), axis=1, keepdims=True)
-    got_bz.append(sum_x(1, got_bx[1]))
+    got_bz = [sum_x(n, got_bx[n]) for n in range(NC)]
     got_cz = [sum_z(n, got_bz[n]) for n in range(NC)]
 
     def columns(piece):
@@ -374,13 +370,11 @@
                 got_y[part][d] = code_y(part, d, value)
             else:
                 wn[rows, :] = value
-            if part == 1 and d == 1:
-                got_z.append(sum_y(0, got_y[0]))
     ht[y] = lax.dot_general(
         jnp.ones((8, 2048), BF), hn[...], (((1,), (1,)), ((), ())), preferred_element_type=F32
     )
     got_h = [send(ht.at[y], ht.at[y], hts.at[d - 1], htr.at[d - 1], at_y(d)) for d in (2, 1, 3)]
-    got_z.append(sum_y(1, got_y[1]))
+    got_z += [sum_y(part, got_y[part]) for part in range(2)]
     for copy in got_h:
         copy.wait_recv()
     hz[zh] = ht[0] + ht[1] + ht[2] + ht[3]
@@ -423,14 +417,19 @@
         given.wait()
 
 
-def hand_on(w_in, h_in, w_out, h_out, sems):
-    copies = [pltpu.make_async_copy(h_in, h_out, sems.at[4])]
+def hand_on(w_in, h_in, w_out, h_out, w_mid, h_mid, sems):
+    moves = [(h_in, h_mid, h_out)]
     for i in range(4):
         rows = pl.ds(i * ROWS, ROWS)
-        copies.append(pltpu.make_async_copy(w_in.at[rows, :], w_out.at[rows, :], sems.at[i]))
-    for copy in copies:
+        moves.append((w_in.at[rows, :], w_mid.at[rows, :], w_out.at[rows, :]))
+    arrive = [pltpu.make_async_copy(src, mid, sems.at[0, i]) for i, (src, mid, dst) in enumerate(moves)]
+    leave = [pltpu.make_async_copy(mid, dst, sems.at[1, i]) for i, (src, mid, dst) in enumerate(moves)]
+    for copy in arrive:
         copy.start()
-    for copy in copies:
+    for before, after in zip(arrive, leave):
+        before.wait()
+        after.start()
+    for copy in leave:
         copy.wait()
 
 
@@ -464,7 +463,7 @@
             dma((2, 3)), dma((2, 3)), dma((2,)), dma((2,)), dma((2, 3)), dma((2, 3)), dma((2, 4)),
         ],
         compiler_params=pltpu.CompilerParams(
-            collective_id=0, has_side_effects=True, vmem_limit_bytes=60 * 1024 * 1024
+            collective_id=0, has_side_effects=True, vmem_limit_bytes=56 * 1024 * 1024
         ),
         name="nmf_update",
     )(counts, w_factor, h_factor)
@@ -473,7 +472,7 @@
         out_shape=shapes,
         in_specs=[far, far],
         out_specs=(far, far),
-        scratch_shapes=[dma((5,))],
+        scratch_shapes=[vmem((960, 128), F32), vmem((2, 2048), F32), dma((2, 5))],
         name="hand_on",
     )(*results)
 

time: 94.2 us -> 79.3 us (0.84)
  the two profiles are of different devices: /device:TPU:8 before, /device:TPU:32 now
where the time goes in v4:
time: 79.3 us; the launch traced here: 79 us
  Pallas kernels  78.4 us (99%)
    pallas_call x1, Pallas kernels, per_device(): pl.pallas_call(kernel, out_shape=shapes, in_specs=[far, far, far], out_sp...  76.6 us
    pallas_call x1, Pallas kernels, per_device(): pl.pallas_call(hand_on, out_shape=shapes, in_specs=[far, far], out_specs=...  1.83 us

profile of v4, /device:TPU:32, one launch (start us, length us, event | category | flops | bytes accessed | tf_op | source)
XLA Modules:
  0.0 79.0 jit_solution(14270695965056026124)
XLA Ops:
  0.6 76.6 %nmf_update.1 = (f32[960,128]{1,0:T(8,128)}, f32[2,2048]{1,0:T(2,128)}) custom-call(bf16[960,2048]{1,0:T(8,128)(2,1)} %cnt_hbm.1, f32[960,128]{1,0:T(8,128)} %w_hbm.1, f32[2,2048]{1,0:T(2,128)} %h_hbm.1), custom_call_target="tpu_custom_call" | custom-call | tf_op jit(solution)/shard_map/nmf_update/pallas_call | solution.py:441
  77.2 1.8 %hand_on.1 = (f32[960,128]{1,0:T(8,128)}, f32[2,2048]{1,0:T(2,128)}) custom-call(f32[960,128]{1,0:T(8,128)} %get-tuple-element.4.w_in, f32[2,2048]{1,0:T(2,128)} %get-tuple-element.5.h_in), custom_call_target="tpu_custom_call" | custom-call | tf_op jit(solution)/shard_map/hand_on/pallas_call | solution.py:470

commit v5 on v4

--- a/solution.py
+++ b/solution.py
@@ -10,7 +10,8 @@
 F32 = jnp.float32
 NC = 2
 CH = 2048 // NC
-ZG = CH // 8
+ZG = CH // 4
+LOW = 2
 HALF = CH // 2
 ROWS = 240
 STARTS, SIZES = (0, 128), (128, 112)
@@ -126,6 +127,31 @@
     for friend in friends:
         pl.semaphore_signal(barrier, inc=1, device_id=friend, device_id_type=MESH)
 
+    is_owner = jnp.logical_and(z >= LOW, z < LOW + 4)
+    mine = jnp.clip(z - LOW, 0, 3)
+    sent_if = []
+
+    def to_owners(src, dst, ssem, rsem):
+        for j in range(4):
+            device = ((LOW + j) * 8 + x * 2 + k, g)
+            copy = remote(src(j), dst, ssem.at[j], rsem.at[z], device)
+            pl.when(z != LOW + j)(copy.start)
+            sent_if.append((z != LOW + j, copy))
+
+    def from_owner(j, src, dst, ssem, rsem):
+        copy = remote(src, dst(j), ssem.at[0], rsem.at[j], at_core)
+        pl.when(z != LOW + j)(copy.wait_recv)
+
+    def to_all(src, dst, ssem, rsem):
+        copies = [remote(src(z_of(d)), dst, ssem.at[d], rsem.at[mine], at_z(d)) for d in FAR]
+
+        @pl.when(is_owner)
+        def _():
+            for copy in copies:
+                copy.start()
+
+        sent_if.extend((is_owner, copy) for copy in copies)
+
     load_h = pltpu.make_async_copy(h_hbm, h_in, ls.at[2])
     load_w = pltpu.make_async_copy(w_hbm, wf, ls.at[1])
     load_cnt = pltpu.make_async_copy(cnt_hbm, cnt, ls.at[0])
@@ -143,13 +169,13 @@
     w_all = wf[...]
     w_sum = jnp.sum(w_all, axis=0, keepdims=True)
     h_own = h_in[...]
-    for zz in range(8):
+    for j in range(4):
         for n in range(NC):
-            base = n * CH + zz * ZG
-            fm[zz, 2 * n : 2 * n + 2, :] = h_own[:, base : base + ZG]
-        fm[zz, 4:5, :] = w_sum
-    got_f = send_z(lambda s: fm.at[s], lambda s: fr.at[s], fs, frs)
-    fr[z] = fm[z]
+            base = n * CH + j * ZG
+            fm[j, 2 * n : 2 * n + 2, :] = h_own[:, base : base + ZG]
+        fm[j, 4:5, :] = jnp.concatenate([w_sum, w_sum], axis=1)
+    to_owners(lambda j: fm.at[j], fr.at[z], fs, frs)
+    fr[z] = fm[mine]
     w_copy = w_all.astype(BF)
     pick = (iota((128, 128), 0) == natural(iota((128, 128), 1))).astype(F32).astype(BF)
     pick_t = (natural(iota((128, 128), 0)) == iota((128, 128), 1)).astype(F32).astype(BF)
@@ -220,33 +246,43 @@
         scale = scale_of(total)
         code = encode(total, scale)
         scale2 = twice(scale)
-        for s in range(8):
+        for s in range(4):
             tz[n, s] = total[:, s * ZG : (s + 1) * ZG]
             bz[n, s, :, 0:ZG] = code[:, s * ZG : (s + 1) * ZG]
             bz[n, s, :, ZG : ZG + 128] = scale2
-        return send_z(lambda s: bz.at[n, s], lambda s: bzr.at[n, s], bzs.at[n], bzrs.at[n])
-
-    def sum_z(n, got):
-        total = tz[n, z]
-        for d in NEAR:
-            s = z_of(d)
-            got[d - 1].wait_recv()
-            total = total + decode(bzr[n, s, :, 0:ZG], bzr[n, s, :, ZG : ZG + 128])
-        updated = h16[n] * total / w_column
-        hu[n] = updated.astype(BF)
-        hmat2[slot, :, genes(n, z)] = hu[n]
-        copies = send_z(lambda s: hu.at[n], lambda s: hmat2.at[slot, :, genes(n, s)], cz.at[n], czr.at[n])
-        for zz in range(8):
-            ho[n, zz] = updated[2 * zz : 2 * zz + 2, :]
-        return copies
+        to_owners(lambda j: bz.at[n, j], bzr.at[n, z], bzs.at[n], bzrs.at[n])
+
+    def sum_z(n):
+        places_z = [z_of(d) for d in NEAR]
+        dues = [remote(bz.at[n, 0], bzr.at[n, s], bzs.at[n, 0], bzrs.at[n, s], at_core) for s in places_z]
+
+        @pl.when(is_owner)
+        def _():
+            total = tz[n, mine]
+            for s, copy in zip(places_z, dues):
+                copy.wait_recv()
+                total = total + decode(bzr[n, s, :, 0:ZG], bzr[n, s, :, ZG : ZG + 128])
+            updated = h16[n] * total / w_column
+            hu[n] = updated.astype(BF)
+            hmat2[slot, :, genes(n, mine)] = hu[n]
+            for zz in range(8):
+                ho[n, zz] = updated[2 * zz : 2 * zz + 2, :]
+            outr[:, genes(n, mine)] = ho[n, z]
+
+        to_all(lambda s: hu.at[n], hmat2.at[slot, :, genes(n, mine)], cz.at[n], czr.at[n])
 
     got = [fan_out(hmat, 0, n, pl.ds(n * CH, CH)) for n in range(NC)]
 
-    for copy in got_f:
-        copy.wait_recv()
+    due_f = [remote(fm.at[0], fr.at[z_of(d)], fs.at[0], frs.at[z_of(d)], at_core) for d in NEAR]
+
+    @pl.when(is_owner)
+    def _():
+        for copy in due_f:
+            copy.wait_recv()
+
     tot = jnp.zeros((1, 128), F32)
     for zz in range(8):
-        tot = tot + fr[zz, 4:5, :]
+        tot = tot + fr[zz, 4:5, 0:128]
         for n in range(NC):
             h16[n, 2 * zz : 2 * zz + 2, :] = fr[zz, 2 * n : 2 * n + 2, :]
     tx[x] = jnp.broadcast_to(tot, (8, 128))
@@ -271,8 +307,10 @@
     places = iota((16, 128), 0)
     own = (places // 2) * 16 + x * 4 + k * 2 + places % 2 == iota((16, 128), 1)
     w_column = jnp.sum(jnp.where(own, w_totals, 0.0), axis=1, keepdims=True)
-    got_bz = [sum_x(n, got_bx[n]) for n in range(NC)]
-    got_cz = [sum_z(n, got_bz[n]) for n in range(NC)]
+    for n in range(NC):
+        sum_x(n, got_bx[n])
+    for n in range(NC):
+        sum_z(n)
 
     def columns(piece):
         at = half if piece < 2 else 1 - half
@@ -281,8 +319,10 @@
     got = []
 
     def z_then_out(piece):
-        for copy in got_cz[piece % 2][0:3] if piece < 2 else got_cz[piece % 2][3:7]:
-            copy.wait_recv()
+        n = piece % 2
+        at = half if piece < 2 else 1 - half
+        for i in range(2):
+            from_owner(2 * at + i, hu.at[n], lambda j: hmat2.at[slot, :, genes(n, j)], cz.at[n], czr.at[n])
         got.append(fan_out(hmat2, 1, piece, columns(piece)))
 
     def pass_on(piece):
@@ -294,10 +334,8 @@
     pass_on(0)
     z_then_out(3)
     pass_on(1)
-    got_o = []
     for n in range(NC):
-        outr[:, genes(n, z)] = ho[n, z]
-        got_o += send_z(lambda s: ho.at[n, s], lambda s: outr.at[:, genes(n, s)], os_.at[n], ors.at[n])
+        to_all(lambda s: ho.at[n, s], outr.at[:, genes(n, mine)], os_.at[n], ors.at[n])
     fan_in(got[0])
     fan_in(got[1])
 
@@ -379,8 +417,9 @@
         copy.wait_recv()
     hz[zh] = ht[0] + ht[1] + ht[2] + ht[3]
     got_hz = send(hz.at[zh], hz.at[zh], hzs.at[0], hzr.at[0], at_zh)
-    for copy in got_o:
-        copy.wait_recv()
+    for n in range(NC):
+        for j in range(4):
+            from_owner(j, ho.at[n, 0], lambda j: outr.at[:, genes(n, j)], os_.at[n], ors.at[n])
     give_h = pltpu.make_async_copy(outr, h_out, ls.at[2])
     give_h.start()
 
@@ -393,8 +432,8 @@
         scale = scale_of(total)
         da[part, y, 0:size, :] = encode(total, scale)
         da[part, y, size : size + 16, :] = twice(scale)
-        mine = da.at[part, y, pl.ds(0, size + 16)]
-        got_w.append({d: send(mine, mine, das.at[part, d - 1], dar.at[part, d - 1], at_y(d)) for d in (2, 1, 3)})
+        code = da.at[part, y, pl.ds(0, size + 16)]
+        got_w.append({d: send(code, code, das.at[part, d - 1], dar.at[part, d - 1], at_y(d)) for d in (2, 1, 3)})
     got_hz.wait_recv()
     h_totals = hz[0] + hz[1]
     gives = [give_h]
@@ -413,6 +452,8 @@
             gives.append(given)
     for copy in sent:
         copy.wait_send()
+    for condition, copy in sent_if:
+        pl.when(condition)(copy.wait_send)
     for given in gives:
         given.wait()
 
@@ -447,11 +488,11 @@
             vmem((960, 2048), BF), vmem((960, 128), F32), vmem((2, 2048), F32), vmem((960, 128), BF), vmem((128, 960), BF),
             vmem((960, CH), BF),
             vmem((2, 2048), BF), vmem((8, 2, 2048), BF), vmem((2, 8, 2048), F32), vmem((8, 16, 2048), BF),
-            vmem((8, 8, 128), F32), vmem((8, 8, 128), F32), vmem((NC, 16, ZG), F32),
+            vmem((4, 8, ZG), F32), vmem((8, 8, ZG), F32), vmem((NC, 16, ZG), F32),
             vmem((4, 8, 128), F32), vmem((2, 8, 128), F32),
             vmem((NC, 2, 64, CH), F32), vmem((NC, 64, CH), F32), vmem((NC, 4, 16, CH), F32),
             vmem((NC, 4, 16, CH + 128), BF), vmem((NC, 3, 16, CH + 128), BF),
-            vmem((NC, 8, 16, ZG), F32), vmem((NC, 8, 16, ZG + 128), BF), vmem((NC, 8, 16, ZG + 128), BF),
+            vmem((NC, 4, 16, ZG), F32), vmem((NC, 4, 16, ZG + 128), BF), vmem((NC, 8, 16, ZG + 128), BF),
             vmem((NC, 16, ZG), BF), vmem((NC, 8, 2, ZG), F32), vmem((2, 2048), F32),
             vmem((8, 16, 2048), BF), vmem((128, 2048), BF), vmem((4, 8, 128), F32), vmem((2, 8, 128), F32),
             vmem((960, 128), F32), vmem((2, 3, 144, 128), BF), vmem((2, 3, 144, 128), BF),

time: 79.3 us -> 77.5 us (0.977)
  Pallas kernels: 78.4 us -> 76.6 us
    pallas_call x1, Pallas kernels: 76.6 us -> 74.7 us  [per_device(): pl.pallas_call(kernel, out_shape=shapes, in_specs=[far, far, far], out_sp...]
where the time goes in v5:
time: 77.5 us; the launch traced here: 77.2 us
  Pallas kernels  76.6 us (99%)
    pallas_call x1, Pallas kernels, per_device(): pl.pallas_call(kernel, out_shape=shapes, in_specs=[far, far, far], out_sp...  74.7 us
    pallas_call x1, Pallas kernels, per_device(): pl.pallas_call(hand_on, out_shape=shapes, in_specs=[far, far], out_specs=...  1.83 us

profile of v5, /device:TPU:32, one launch (start us, length us, event | category | flops | bytes accessed | tf_op | source)
XLA Modules:
  0.0 77.2 jit_solution(15340329713237191320)
XLA Ops:
  0.6 74.7 %nmf_update.1 = (f32[960,128]{1,0:T(8,128)}, f32[2,2048]{1,0:T(2,128)}) custom-call(bf16[960,2048]{1,0:T(8,128)(2,1)} %cnt_hbm.1, f32[960,128]{1,0:T(8,128)} %w_hbm.1, f32[2,2048]{1,0:T(2,128)} %h_hbm.1), custom_call_target="tpu_custom_call" | custom-call | tf_op jit(solution)/shard_map/nmf_update/pallas_call | solution.py:482
  75.4 1.8 %hand_on.1 = (f32[960,128]{1,0:T(8,128)}, f32[2,2048]{1,0:T(2,128)}) custom-call(f32[960,128]{1,0:T(8,128)} %get-tuple-element.4.w_in, f32[2,2048]{1,0:T(2,128)} %get-tuple-element.5.h_in), custom_call_target="tpu_custom_call" | custom-call | tf_op jit(solution)/shard_map/hand_on/pallas_call | solution.py:511

commit v6 on v5

--- a/solution.py
+++ b/solution.py
@@ -10,8 +10,9 @@
 F32 = jnp.float32
 NC = 2
 CH = 2048 // NC
-ZG = CH // 4
-LOW = 2
+OWNERS = 2
+ZG = CH // OWNERS
+LOW = 3
 HALF = CH // 2
 ROWS = 240
 STARTS, SIZES = (0, 128), (128, 112)
@@ -127,12 +128,12 @@
     for friend in friends:
         pl.semaphore_signal(barrier, inc=1, device_id=friend, device_id_type=MESH)
 
-    is_owner = jnp.logical_and(z >= LOW, z < LOW + 4)
-    mine = jnp.clip(z - LOW, 0, 3)
+    is_owner = jnp.logical_and(z >= LOW, z < LOW + OWNERS)
+    mine = jnp.clip(z - LOW, 0, OWNERS - 1)
     sent_if = []
 
     def to_owners(src, dst, ssem, rsem):
-        for j in range(4):
+        for j in range(OWNERS):
             device = ((LOW + j) * 8 + x * 2 + k, g)
             copy = remote(src(j), dst, ssem.at[j], rsem.at[z], device)
             pl.when(z != LOW + j)(copy.start)
@@ -169,11 +170,11 @@
     w_all = wf[...]
     w_sum = jnp.sum(w_all, axis=0, keepdims=True)
     h_own = h_in[...]
-    for j in range(4):
+    for j in range(OWNERS):
         for n in range(NC):
             base = n * CH + j * ZG
             fm[j, 2 * n : 2 * n + 2, :] = h_own[:, base : base + ZG]
-        fm[j, 4:5, :] = jnp.concatenate([w_sum, w_sum], axis=1)
+        fm[j, 4:5, :] = jnp.concatenate([w_sum] * (ZG // 128), axis=1)
     to_owners(lambda j: fm.at[j], fr.at[z], fs, frs)
     fr[z] = fm[mine]
     w_copy = w_all.astype(BF)
@@ -246,7 +247,7 @@
         scale = scale_of(total)
         code = encode(total, scale)
         scale2 = twice(scale)
-        for s in range(4):
+        for s in range(OWNERS):
             tz[n, s] = total[:, s * ZG : (s + 1) * ZG]
             bz[n, s, :, 0:ZG] = code[:, s * ZG : (s + 1) * ZG]
             bz[n, s, :, ZG : ZG + 128] = scale2
@@ -321,8 +322,8 @@
     def z_then_out(piece):
         n = piece % 2
         at = half if piece < 2 else 1 - half
-        for i in range(2):
-            from_owner(2 * at + i, hu.at[n], lambda j: hmat2.at[slot, :, genes(n, j)], cz.at[n], czr.at[n])
+        for i in range(OWNERS // 2):
+            from_owner(OWNERS // 2 * at + i, hu.at[n], lambda j: hmat2.at[slot, :, genes(n, j)], cz.at[n], czr.at[n])
         got.append(fan_out(hmat2, 1, piece, columns(piece)))
 
     def pass_on(piece):
@@ -418,7 +419,7 @@
     hz[zh] = ht[0] + ht[1] + ht[2] + ht[3]
     got_hz = send(hz.at[zh], hz.at[zh], hzs.at[0], hzr.at[0], at_zh)
     for n in range(NC):
-        for j in range(4):
+        for j in range(OWNERS):
             from_owner(j, ho.at[n, 0], lambda j: outr.at[:, genes(n, j)], os_.at[n], ors.at[n])
     give_h = pltpu.make_async_copy(outr, h_out, ls.at[2])
     give_h.start()
@@ -488,11 +489,11 @@
             vmem((960, 2048), BF), vmem((960, 128), F32), vmem((2, 2048), F32), vmem((960, 128), BF), vmem((128, 960), BF),
             vmem((960, CH), BF),
             vmem((2, 2048), BF), vmem((8, 2, 2048), BF), vmem((2, 8, 2048), F32), vmem((8, 16, 2048), BF),
-            vmem((4, 8, ZG), F32), vmem((8, 8, ZG), F32), vmem((NC, 16, ZG), F32),
+            vmem((OWNERS, 8, ZG), F32), vmem((8, 8, ZG), F32), vmem((NC, 16, ZG), F32),
             vmem((4, 8, 128), F32), vmem((2, 8, 128), F32),
             vmem((NC, 2, 64, CH), F32), vmem((NC, 64, CH), F32), vmem((NC, 4, 16, CH), F32),
             vmem((NC, 4, 16, CH + 128), BF), vmem((NC, 3, 16, CH + 128), BF),
-            vmem((NC, 4, 16, ZG), F32), vmem((NC, 4, 16, ZG + 128), BF), vmem((NC, 8, 16, ZG + 128), BF),
+            vmem((NC, OWNERS, 16, ZG), F32), vmem((NC, OWNERS, 16, ZG + 128), BF), vmem((NC, 8, 16, ZG + 128), BF),
             vmem((NC, 16, ZG), BF), vmem((NC, 8, 2, ZG), F32), vmem((2, 2048), F32),
             vmem((8, 16, 2048), BF), vmem((128, 2048), BF), vmem((4, 8, 128), F32), vmem((2, 8, 128), F32),
             vmem((960, 128), F32), vmem((2, 3, 144, 128), BF), vmem((2, 3, 144, 128), BF),

time: 77.5 us -> 78.2 us (level)
  the two profiles are of different devices: /device:TPU:32 before, /device:TPU:2 now
where the time goes in v6:
time: 78.2 us; the launch traced here: 77.9 us
  Pallas kernels  77.3 us (99%)
    pallas_call x1, Pallas kernels, per_device(): pl.pallas_call(kernel, out_shape=shapes, in_specs=[far, far, far], out_sp...  75.5 us
    pallas_call x1, Pallas kernels, per_device(): pl.pallas_call(hand_on, out_shape=shapes, in_specs=[far, far], out_specs=...  1.83 us

profile of v6, /device:TPU:2, one launch (start us, length us, event | category | flops | bytes accessed | tf_op | source)
XLA Modules:
  0.0 77.9 jit_solution(2105761963402226785)
XLA Ops:
  0.6 75.5 %nmf_update.1 = (f32[960,128]{1,0:T(8,128)}, f32[2,2048]{1,0:T(2,128)}) custom-call(bf16[960,2048]{1,0:T(8,128)(2,1)} %cnt_hbm.1, f32[960,128]{1,0:T(8,128)} %w_hbm.1, f32[2,2048]{1,0:T(2,128)} %h_hbm.1), custom_call_target="tpu_custom_call" | custom-call | tf_op jit(solution)/shard_map/nmf_update/pallas_call | solution.py:483
  76.1 1.8 %hand_on.1 = (f32[960,128]{1,0:T(8,128)}, f32[2,2048]{1,0:T(2,128)}) custom-call(f32[960,128]{1,0:T(8,128)} %get-tuple-element.4.w_in, f32[2,2048]{1,0:T(2,128)} %get-tuple-element.5.h_in), custom_call_target="tpu_custom_call" | custom-call | tf_op jit(solution)/shard_map/hand_on/pallas_call | solution.py:512

commit v7 on v5

--- a/solution.py
+++ b/solution.py
@@ -122,8 +122,8 @@
         ]
 
     barrier = pltpu.get_barrier_semaphore()
-    friends = [at_z(d) for d in FAR] + [at_x(d) for d in range(1, 4)] + [at_core]
-    friends += [at_y(d) for d in range(1, 4)] + [at_zh]
+    friends = [at_zh] + [at_z(d) for d in FAR] + [at_x(d) for d in range(1, 4)] + [at_core]
+    friends += [at_y(d) for d in range(1, 4)]
     for friend in friends:
         pl.semaphore_signal(barrier, inc=1, device_id=friend, device_id_type=MESH)
 
@@ -412,6 +412,7 @@
         jnp.ones((8, 2048), BF), hn[...], (((1,), (1,)), ((), ())), preferred_element_type=F32
     )
     got_h = [send(ht.at[y], ht.at[y], hts.at[d - 1], htr.at[d - 1], at_y(d)) for d in (2, 1, 3)]
+    early = list(sent)
     got_z += [sum_y(part, got_y[part]) for part in range(2)]
     for copy in got_h:
         copy.wait_recv()
@@ -420,6 +421,10 @@
     for n in range(NC):
         for j in range(4):
             from_owner(j, ho.at[n, 0], lambda j: outr.at[:, genes(n, j)], os_.at[n], ors.at[n])
+    for copy in early:
+        copy.wait_send()
+    for condition, copy in sent_if:
+        pl.when(condition)(copy.wait_send)
     give_h = pltpu.make_async_copy(outr, h_out, ls.at[2])
     give_h.start()
 
@@ -450,10 +455,8 @@
             given = pltpu.make_async_copy(wv.at[rows, :], w_out.at[rows, :], gs.at[part, d])
             given.start()
             gives.append(given)
-    for copy in sent:
+    for copy in sent[len(early) :]:
         copy.wait_send()
-    for condition, copy in sent_if:
-        pl.when(condition)(copy.wait_send)
     for given in gives:
         given.wait()
 

time: 77.5 us -> 77.5 us (level)
  no operation moved by 1% of the time
where the time goes in v7:
time: 77.5 us; the launch traced here: 77.2 us
  Pallas kernels  76.5 us (99%)
    pallas_call x1, Pallas kernels, per_device(): pl.pallas_call(kernel, out_shape=shapes, in_specs=[far, far, far], out_sp...  74.7 us
    pallas_call x1, Pallas kernels, per_device(): pl.pallas_call(hand_on, out_shape=shapes, in_specs=[far, far], out_specs=...  1.83 us

profile of v7, /device:TPU:32, one launch (start us, length us, event | category | flops | bytes accessed | tf_op | source)
XLA Modules:
  0.0 77.2 jit_solution(10149168841345399478)
XLA Ops:
  0.6 74.7 %nmf_update.1 = (f32[960,128]{1,0:T(8,128)}, f32[2,2048]{1,0:T(2,128)}) custom-call(bf16[960,2048]{1,0:T(8,128)(2,1)} %cnt_hbm.1, f32[960,128]{1,0:T(8,128)} %w_hbm.1, f32[2,2048]{1,0:T(2,128)} %h_hbm.1), custom_call_target="tpu_custom_call" | custom-call | tf_op jit(solution)/shard_map/nmf_update/pallas_call | solution.py:485
  75.3 1.8 %hand_on.1 = (f32[960,128]{1,0:T(8,128)}, f32[2,2048]{1,0:T(2,128)}) custom-call(f32[960,128]{1,0:T(8,128)} %get-tuple-element.4.w_in, f32[2,2048]{1,0:T(2,128)} %get-tuple-element.5.h_in), custom_call_target="tpu_custom_call" | custom-call | tf_op jit(solution)/shard_map/hand_on/pallas_call | solution.py:514
